TPU v7x, 32 devices: a whole 2x2x4 slice. The times are simulated.
32 devices in a mesh: bead: 8 (over y, x, core), atom: 4 (over z).
Axes of the slice: x: 2, y: 2, z: 4, core: 2. Of those that a mesh axis runs over, the one named last changes fastest.
Arguments:
- positions: float32 [3, 8, 1024], P(None, 'bead', 'atom'), may hold values from -1 to 11, as said below
- velocities: float32 [3, 8, 1024], P(None, 'bead', 'atom'), may hold values from -3 to 3
- forces_now: float32 [3, 8, 1024], P(None, 'bead', 'atom'), may hold values from -18 to 18
- masses: float32 [1024], P('atom'), may hold values from 1 to 16
- features: bfloat16 [8, 256, 1024], P('bead', None, 'atom'), may hold values from -6 to 6
- tile_blocks: int32 [8, 9], P('atom'), may hold values from 0 to 7, as said below
- block_slots: int32 [1024], P('atom'), may hold values from 0 to 1023, as said below
- w_basis: bfloat16 [64, 32], replicated, may hold values from -1 to 1
- w_feat: bfloat16 [64, 256], replicated, may hold values from -0.375 to 0.375
- hidden_bias: float32 [64], replicated, may hold values from -5 to 5
- w_out: float32 [64], replicated, may hold values from -0.03 to 0.03
Outputs:
- positions_next: float32 [3, 8, 1024], P(None, 'bead', 'atom')
- velocities_next: float32 [3, 8, 1024], P(None, 'bead', 'atom')
- forces_next: float32 [3, 8, 1024], P(None, 'bead', 'atom')
Inputs may be any that keep to these rules, and one draw needn't show every extreme that they name: `tile_blocks`: every entry of row k is one of the blocks k - 4 to k + 4, counted cyclically over the 8 blocks; blocks k - 4 and k + 4 are always named; the other entries may repeat; the order is drawn for each row. `block_slots`: the entries j * 256 to (j + 1) * 256 - 1 are a permutation of the atom numbers j * 256 to (j + 1) * 256 - 1. `positions`: the beads of one atom lie within 0.06, in each coordinate, of a common centre whose first two coordinates lie in [0, 2.9) and whose third lies in [0.15 k, 0.15 (k + 1)), k the block of the atom's slot.
All inputs are finite; a program needn't handle non-finite values.
Results may differ from a plain program's by a relative error of at most 0.0003.
Values may be sent and summed in bfloat16 or wider, within the bound.
A program may use at most 128 MiB of HBM per device.

v0:
```python
import functools

import jax
import jax.numpy as jnp
from jax import lax
from jax.experimental import pallas as pl
from jax.experimental.pallas import tpu as pltpu
from jax.sharding import PartitionSpec as P

TILE = 128
LAYER_WIDTH = 0.15
SIDE_LENGTH = 2.9
CUTOFF = 0.6
BASIS_SHARPNESS = 355.0
SOFTEN = 0.0001
TIME_STEP = 0.1
OMEGA_SQ = 100.0
REACH_BLOCKS = 4
SLOT = 16
SEGS = TILE // SLOT
LROWS = TILE // SEGS
STACK = 4
MESH = pl.DeviceIdType.MESH
f32, bf16, i32 = jnp.float32, jnp.bfloat16, jnp.int32


def iota(shape, dim):
    return lax.broadcasted_iota(i32, shape, dim)


def dot(a, b, dims=((1,), (0,)), exact=False):
    return lax.dot_general(
        a,
        b,
        (dims, ((), ())),
        precision=lax.Precision.HIGHEST if exact else None,
        preferred_element_type=f32,
    )


def split3(x):
    hi = x.astype(bf16)
    rest = x - hi.astype(f32)
    mid = rest.astype(bf16)
    low = (rest - mid.astype(f32)).astype(bf16)
    return hi, mid, low


def window(blocks_here, shards):
    reach = (REACH_BLOCKS + blocks_here - 1) // blocks_here
    span = min(2 * reach + 1, shards)
    return span, -(span // 2)


def one_hot_slots(slots_ref, shard, atoms):
    local = slots_ref[...] - shard * atoms
    return jnp.where(iota((atoms, atoms), 0) == local, 1.0, 0.0)


def exchange_kernel(
    shards, beads, span, first,
    pos_ref, vel_ref, force_ref, mass_ref, feat_ref, slots_ref, w_feat_ref, wb_ref, wo_ref,
    rim_ref, state_ref, fwd, bwd, read,
    mine, sides, send_sems, recv_sems, bead_send, bead_recv,
):
    atoms = mass_ref.shape[1]
    hid = w_feat_ref.shape[0]
    atom, bead = lax.axis_index("atom"), lax.axis_index("bead")
    rels = [r for r in range(first, first + span) if r != 0]

    def peer(rel):
        return (bead, lax.rem(atom + rel + shards, shards))

    def side(step):
        return (lax.rem(bead + step + beads, beads), atom)

    barrier = pltpu.get_barrier_semaphore()
    for rel in rels:
        pl.semaphore_signal(barrier, inc=1, device_id=peer(rel), device_id_type=MESH)
    for step in (1, -1):
        pl.semaphore_signal(barrier, inc=1, device_id=side(step), device_id_type=MESH)

    half = vel_ref[:, 0, :] + (0.5 * TIME_STEP) * force_ref[:, 0, :] / mass_ref[...]
    moved = pos_ref[:, 0, :] + TIME_STEP * half
    mine[0:3, :] = moved
    mine[3:8, :] = jnp.zeros((5, atoms), f32)
    hot = one_hot_slots(slots_ref, atom, atoms).astype(bf16)
    projected = dot(w_feat_ref[...], feat_ref[0]).astype(bf16)
    sorted_proj = dot(projected, hot).astype(bf16)
    parts = jnp.concatenate([p.astype(f32) for p in split3(moved)] + [jnp.zeros((7, atoms), f32)], axis=0)
    sorted_pos = dot(parts.astype(bf16), hot).astype(bf16)
    own = -first
    rim_ref[own, 0:hid, :] = sorted_proj
    rim_ref[own, hid : hid + 16, :] = sorted_pos
    pl.semaphore_wait(barrier, len(rels) + 2)

    bead_copies = []
    for k, step in enumerate((1, -1)):
        copy = pltpu.make_async_remote_copy(
            src_ref=mine, dst_ref=sides.at[k], send_sem=bead_send.at[k],
            recv_sem=bead_recv.at[k], device_id=side(step), device_id_type=MESH,
        )
        copy.start()
        bead_copies.append(copy)

    copies = []
    for rel in rels:
        slot = rel - first
        copy = pltpu.make_async_remote_copy(
            src_ref=rim_ref.at[own], dst_ref=rim_ref.at[slot], send_sem=send_sems.at[slot],
            recv_sem=recv_sems.at[slot], device_id=peer(-rel), device_id_type=MESH,
        )
        copy.start()
        copies.append(copy)
    nb = wb_ref.shape[0]
    up, dn = STACK * hid, STACK * nb
    take_h = jnp.where(lax.rem(iota((up, hid), 0), hid) == iota((up, hid), 1), 1.0, 0.0)
    take_j = jnp.where(lax.rem(iota((dn, nb), 0), nb) == iota((dn, nb), 1), 1.0, 0.0).astype(bf16)
    wb = wb_ref[...]
    wide = dot(dot(take_h.astype(bf16), wb, ((1,), (1,))).astype(bf16), take_j, ((1,), (1,)))
    fwd[...] = jnp.where(iota((up, dn), 0) // hid == iota((up, dn), 1) // nb, wide, 0.0).astype(bf16)
    scaled = (wb.astype(f32) * wo_ref[...]).astype(bf16)
    back = dot(dot(take_j, scaled).astype(bf16), take_h.astype(bf16), ((1,), (1,)))
    bwd[...] = jnp.where(iota((dn, up), 0) // nb == iota((dn, up), 1) // hid, back, 0.0).astype(bf16)
    wo_all = jnp.broadcast_to(wo_ref[...].astype(bf16), (16, hid))
    outs = dot(wo_all, take_h.astype(bf16), ((1,), (1,)))
    read[...] = jnp.where(iota((16, up), 0) == iota((16, up), 1) // hid, outs, 0.0).astype(bf16)
    for copy in bead_copies:
        copy.wait()
    spring = -OMEGA_SQ * mass_ref[...] * (2.0 * moved - sides[0, 0:3, :] - sides[1, 0:3, :])
    state_ref[0] = moved
    state_ref[1] = half
    state_ref[2] = spring
    for copy in copies:
        copy.wait()


def lanes_of(table, index):
    return jnp.take_along_axis(table, index, axis=1, mode="promise_in_bounds")


def column_of(row):
    n = row.shape[1]
    eye = iota((n, n), 0) == iota((n, n), 1)
    return jnp.sum(jnp.where(eye, row, 0.0), axis=1, keepdims=True)


def wrapped(c, box):
    return c - box * jnp.floor(c / box + 0.5)


def pair_kernel(
    shards, span, first, named,
    tiles_ref, rim_ref, state_ref, mass_ref, slots_ref, fwd, bwd, read, bias_ref,
    pos_out, vel_out, force_out,
    pos_all, proj_all, spread, row_cols, row_terms, packed, acc, sums, dist_ref, pair_ref, energy_ref, slope_ref,
    entry_count, entry_blk, entry_tile, jobs,
):
    atoms = mass_ref.shape[1]
    hid = bias_ref.shape[1]
    nb = bwd.shape[0] // STACK
    here = atoms // TILE
    blocks_all = here * shards
    boxes = (SIDE_LENGTH, SIDE_LENGTH, blocks_all * LAYER_WIDTH)
    atom = lax.axis_index("atom")
    own = -first * here

    bias = column_of(bias_ref[...])
    centres = CUTOFF * (lax.rem(iota((STACK * nb, TILE), 0), nb).astype(f32) + 0.5) / nb
    for c in range(span):
        parts = rim_ref[c, hid : hid + 16, :].astype(f32)
        whole = parts[0:3] + (parts[3:6] + parts[6:9])
        proj = rim_ref[c, 0:hid, :].astype(f32)
        for b in range(here):
            pos_all[c * here + b, 0:3, :] = whole[:, b * TILE : (b + 1) * TILE]
            proj_all[c * here + b] = proj[:, b * TILE : (b + 1) * TILE]
    before = jnp.where(iota((TILE, TILE), 0) < iota((TILE, TILE), 1), 1.0, 0.0).astype(bf16)
    lane = iota((TILE, TILE), 1)
    row = iota((TILE, TILE), 0)
    seg = iota((LROWS, TILE), 1) // SLOT
    row_of = LROWS * seg + iota((LROWS, TILE), 0)

    for blk in range(here):
        rows_pos = pos_all[own + blk]
        for d in range(3):
            row_cols[blk * 3 + d] = jnp.broadcast_to(column_of(rows_pos[d : d + 1]), (TILE, TILE))
            spread[blk * 3 + d] = lanes_of(jnp.broadcast_to(rows_pos[d : d + 1], (LROWS, TILE)), row_of)
        rows_proj = proj_all[own + blk] + bias
        for q in range(LROWS):
            row_terms[blk * LROWS + q] = lanes_of(rows_proj, jnp.broadcast_to(row_of[q : q + 1], (hid, TILE)))
    acc[...] = jnp.zeros_like(acc)

    def list_entry(at, n):
        blk, l = at // (span * here), lax.rem(at, span * here)
        block_id = lax.rem((atom + first) * here + l + blocks_all * 2, blocks_all)
        count = jnp.int32(0)
        for k in range(named):
            count += jnp.where(tiles_ref[blk, k] == block_id, 1, 0).astype(i32)
        entry_count[n] = count
        entry_blk[n] = blk
        entry_tile[n] = l
        return n + jnp.where(count > 0, 1, 0).astype(i32)

    entries = lax.fori_loop(0, here * span * here, list_entry, jnp.int32(0))
    entry_count[entries] = 0
    entry_blk[entries] = 0
    entry_tile[entries] = 0
    packed[entries] = jnp.zeros((TILE, TILE), i32)

    def compact(e):
        blk, l = entry_blk[e], entry_tile[e]
        cols_pos = pos_all[l]
        dist_sq = None
        for d in range(3):
            c = cols_pos[d : d + 1] - row_cols[blk * 3 + d]
            c = c - boxes[d] * jnp.floor(c * (1.0 / boxes[d]) + 0.5)
            dist_sq = c * c if dist_sq is None else dist_sq + c * c
        limit = jnp.where(entry_count[e] > 0, CUTOFF * CUTOFF + 1e-3, -1.0).astype(f32)
        near = (dist_sq < limit) & (row - lane != jnp.where(l == own + blk, 0, 2 * TILE))
        marks = jnp.where(near, 1.0, 0.0)
        ahead = dot(marks.astype(bf16), before)
        most = jnp.max(ahead[:, TILE - 1 :] + marks[:, TILE - 1 :]).astype(i32)
        x = jnp.where(near, (lane - ahead.astype(i32)) * 256 + lane + 128, 0)
        step = 1
        while step < TILE:
            bit = step * 256
            come = pltpu.roll(x, TILE - step, 1)
            x = jnp.where((come & bit) != 0, come, jnp.where((x & bit) != 0, 0, x))
            step *= 2
        packed[e] = x & 255
        return most

    def list_jobs(it, n):
        mosts = [compact(2 * it + u) for u in range(2)]
        for u in range(2):
            turns = (mosts[u] + SLOT - 1) // SLOT

            def add(turn, _, u=u, n=n):
                jobs[n + turn] = (2 * it + u) * SEGS + turn
                return 0

            lax.fori_loop(0, turns, add, 0)
            n = n + turns
        return n

    total = lax.fori_loop(0, (entries + 1) // 2, list_jobs, jnp.int32(0))
    jobs[total] = entries * SEGS

    def one_job(u, job):
        e, turn = job // SEGS, lax.rem(job, SEGS)
        blk, l = entry_blk[e], entry_tile[e]
        code = None
        for i in range(SEGS):
            part = packed[e, i * LROWS : (i + 1) * LROWS, :]
            part = pltpu.roll(part, lax.rem((i - turn) * SLOT + TILE, TILE), 1)
            code = part if code is None else jnp.where(seg == i, part, code)
        live = code >= 128
        index = code & 127
        disp = []
        dist_sq = None
        for d in range(3):
            c = lanes_of(jnp.broadcast_to(pos_all[l, d : d + 1, :], (LROWS, TILE)), index)
            c = wrapped(c - spread[blk * 3 + d], boxes[d])
            disp.append(c)
            dist_sq = c * c if dist_sq is None else dist_sq + c * c
        distance = jnp.sqrt(dist_sq + SOFTEN)
        dist_ref[u] = distance
        pair_ref[u] = index
        cols_proj = proj_all[l]
        for half in range(LROWS // (2 * STACK)):
            offs, vals, terms = [], [], []
            for g in range(2):
                base = (2 * half + g) * STACK
                rows = range(base, base + STACK)
                off = jnp.concatenate(
                    [jnp.broadcast_to(dist_ref[u, q : q + 1, :], (nb, TILE)) for q in rows], axis=0
                ) - centres
                val = jnp.exp(-BASIS_SHARPNESS * off * off)
                vals.append(val.astype(bf16))
                offs.append(off * val)
                terms.append(
                    jnp.concatenate(
                        [
                            row_terms[blk * LROWS + q]
                            + lanes_of(cols_proj, jnp.broadcast_to(pair_ref[u, q : q + 1, :], (hid, TILE)))
                            for q in rows
                        ],
                        axis=0,
                    )
                )
            pre = dot(fwd[...], jnp.concatenate(vals, axis=1)) + jnp.concatenate(terms, axis=1)
            act = jnp.tanh(pre.astype(bf16))
            energy = dot(read[...], act)
            grad = dot(bwd[...], 1.0 - act * act)
            for g in range(2):
                base = (2 * half + g) * STACK
                part = grad[:, g * TILE : (g + 1) * TILE] * offs[g]
                energy_ref[u, base : base + STACK, :] = energy[0:STACK, g * TILE : (g + 1) * TILE]
                for r in range(STACK):
                    slope_ref[u, base + r : base + r + 1, :] = jnp.sum(
                        part[r * nb : (r + 1) * nb], axis=0, keepdims=True
                    )
        inner = jnp.maximum(1.0 - dist_sq / (CUTOFF * CUTOFF), 0.0)
        de_ds = (-2.0 * inner / (CUTOFF * CUTOFF)) * energy_ref[u] + inner * inner * (
            -BASIS_SHARPNESS * slope_ref[u] / distance
        )
        scale = jnp.where(live, de_ds, 0.0) * (2.0 * entry_count[e].astype(f32))
        return blk, [scale * c for c in disp]

    def job_pair(it, _):
        done = [one_job(u, jobs[2 * it + u]) for u in range(2)]
        for blk, forces in done:
            for d in range(3):
                acc[blk * 3 + d] += forces[d]
        return 0

    lax.fori_loop(0, (total + 1) // 2, job_pair, 0)

    seg_sum = jnp.where(row // SLOT == lane // LROWS, 1.0, 0.0)
    mine = lax.rem(iota((LROWS, TILE), 1), LROWS) == iota((LROWS, TILE), 0)
    sums[...] = jnp.zeros_like(sums)
    for blk in range(here):
        for d in range(3):
            s = dot(acc[blk * 3 + d], seg_sum, exact=True)
            sums[d : d + 1, blk * TILE : (blk + 1) * TILE] = jnp.sum(
                jnp.where(mine, s, 0.0), axis=0, keepdims=True
            )
    hot = one_hot_slots(slots_ref, atom, atoms)
    pair = dot(sums[...], hot, ((1,), (1,)), exact=True)[0:3]
    moved, half, spring = state_ref[0], state_ref[1], state_ref[2]
    force = pair + spring
    pos_out[:, 0, :] = moved
    force_out[:, 0, :] = force
    vel_out[:, 0, :] = half + (0.5 * TIME_STEP) * force / mass_ref[...]


def body(
    positions, velocities, forces_now, masses, features, tile_blocks, block_slots,
    w_basis, w_feat, hidden_bias, w_out,
):
    atoms = positions.shape[2]
    hid, nb = w_basis.shape
    here = atoms // TILE
    shards, beads = lax.axis_size("atom"), lax.axis_size("bead")
    span, first = window(here, shards)
    mass_row = masses.reshape(1, atoms)
    slot_row = block_slots.reshape(1, atoms)
    vmem = pl.BlockSpec(memory_space=pltpu.VMEM)
    rim, state, fwd, bwd, read = pl.pallas_call(
        functools.partial(exchange_kernel, shards, beads, span, first),
        out_shape=(
            jax.ShapeDtypeStruct((span, hid + 16, atoms), bf16),
            jax.ShapeDtypeStruct((3, 3, atoms), f32),
            jax.ShapeDtypeStruct((STACK * hid, STACK * nb), bf16),
            jax.ShapeDtypeStruct((STACK * nb, STACK * hid), bf16),
            jax.ShapeDtypeStruct((16, STACK * hid), bf16),
        ),
        in_specs=[vmem] * 9,
        out_specs=(vmem,) * 5,
        scratch_shapes=[
            pltpu.VMEM((8, atoms), f32),
            pltpu.VMEM((2, 8, atoms), f32),
            pltpu.SemaphoreType.DMA((span,)),
            pltpu.SemaphoreType.DMA((span,)),
            pltpu.SemaphoreType.DMA((2,)),
            pltpu.SemaphoreType.DMA((2,)),
        ],
        compiler_params=pltpu.CompilerParams(collective_id=0, has_side_effects=True),
        name="exchange",
    )(positions, velocities, forces_now, mass_row, features, slot_row, w_feat, w_basis.T, w_out.reshape(1, hid))
    out = jax.ShapeDtypeStruct(positions.shape, f32)
    entries = here * span * here + 2
    return pl.pallas_call(
        functools.partial(pair_kernel, shards, span, first, tile_blocks.shape[1]),
        out_shape=(out, out, out),
        in_specs=[pl.BlockSpec(memory_space=pltpu.SMEM)] + [vmem] * 8,
        out_specs=(vmem, vmem, vmem),
        scratch_shapes=[
            pltpu.VMEM((span * here, 8, TILE), f32),
            pltpu.VMEM((span * here, hid, TILE), f32),
            pltpu.VMEM((here * 3, LROWS, TILE), f32),
            pltpu.VMEM((here * 3, TILE, TILE), f32),
            pltpu.VMEM((here * LROWS, hid, TILE), f32),
            pltpu.VMEM((entries, TILE, TILE), i32),
            pltpu.VMEM((here * 3, LROWS, TILE), f32),
            pltpu.VMEM((8, atoms), f32),
            pltpu.VMEM((2, LROWS, TILE), f32),
            pltpu.VMEM((2, LROWS, TILE), i32),
            pltpu.VMEM((2, LROWS, TILE), f32),
            pltpu.VMEM((2, LROWS, TILE), f32),
            pltpu.SMEM((entries,), i32),
            pltpu.SMEM((entries,), i32),
            pltpu.SMEM((entries,), i32),
            pltpu.SMEM((entries * SEGS + 2,), i32),
        ],
        compiler_params=pltpu.CompilerParams(vmem_limit_bytes=32 * 1024 * 1024),
        name="pairs",
    )(
        tile_blocks, rim, state, mass_row, slot_row, fwd, bwd, read,
        hidden_bias.reshape(1, hid),
    )


def solution(mesh):
    vec = P(None, "bead", "atom")
    return jax.shard_map(
        body,
        mesh=mesh,
        in_specs=(
            vec, vec, vec, P("atom"), P("bead", None, "atom"), P("atom", None), P("atom"),
            P(), P(), P(), P(),
        ),
        out_specs=(vec, vec, vec),
        check_vma=False,
    )
```

profile of v0, /device:TPU:8, one launch (start us, length us, event | category | flops | bytes accessed | tf_op | source)
XLA Modules:
  0.0 34.1 jit_solution(15479880353857296469)
XLA Ops:
  0.6 0.0 copy-start.6
  0.6 0.0 copy-start.7
  0.7 0.0 copy-start.8
  0.7 9.5 %exchange.1 = (bf16[4,80,256]{2,1,0:T(8,128)(2,1)}, f32[3,3,256]{2,1,0:T(4,128)}, bf16[256,128]{1,0:T(8,128)(2,1)}, bf16[128,256]{1,0:T(8,128)(2,1)}, bf16[16,256]{1,0:T(8,128)(2,1)}) custom-call(f32[3,1,256]{2,1,0:T(1,128)} %pos_ref.1, f32[3,1,256]{2,1,0:T(1,128)} %vel_ref.1, f32[3,1,256]{2,1,0:T(1,128)} %force_ref.1, f32[1,256]{1,0:T(1,128)} %bitcast.5, ...), custom_call_target="tpu_custom_call" | custom-call | tf_op jit(solution)/shard_map/exchange/pallas_call | solution.py:349
  10.2 0.0 copy-start.4
  10.2 0.0 copy-start.5
  10.2 0.0 copy-done.6
  10.2 0.0 copy-done.7
  10.2 0.0 copy-done.8
  10.2 0.6 %copy-done.4 = bf16[16,256]{1,0:T(8,128)(2,1)S(1)} copy-done((bf16[16,256]{1,0:T(8,128)(2,1)S(1)}, bf16[16,256]{1,0:T(8,128)(2,1)}, u32[]{:S(2)}) %copy-start.4) | copy-done | bytes 8216
  10.9 0.0 copy-done.5
  10.9 0.0 copy-start
  10.9 0.9 %copy-done = bf16[4,80,256]{2,1,0:T(8,128)(2,1)S(1)} copy-done((bf16[4,80,256]{2,1,0:T(8,128)(2,1)S(1)}, bf16[4,80,256]{2,1,0:T(8,128)(2,1)}, u32[]{:S(2)}) %copy-start) | copy-done | bytes 163864
  11.8 0.0 copy-start.1
  11.8 0.8 %copy-done.1 = bf16[256,128]{1,0:T(8,128)(2,1)S(1)} copy-done((bf16[256,128]{1,0:T(8,128)(2,1)S(1)}, bf16[256,128]{1,0:T(8,128)(2,1)}, u32[]{:S(2)}) %copy-start.1) | copy-done | bytes 65560
  12.6 0.0 copy-start.2
  12.6 0.8 %copy-done.2 = bf16[128,256]{1,0:T(8,128)(2,1)S(1)} copy-done((bf16[128,256]{1,0:T(8,128)(2,1)S(1)}, bf16[128,256]{1,0:T(8,128)(2,1)}, u32[]{:S(2)}) %copy-start.2) | copy-done | bytes 65560
  13.5 0.0 copy-start.3
  13.5 0.7 %copy-done.3 = f32[3,3,256]{2,1,0:T(4,128)S(1)} copy-done((f32[3,3,256]{2,1,0:T(4,128)S(1)}, f32[3,3,256]{2,1,0:T(4,128)}, u32[]{:S(2)}) %copy-start.3) | copy-done | bytes 9240
  14.2 19.9 %pairs.1 = (f32[3,1,256]{2,1,0:T(1,128)}, f32[3,1,256]{2,1,0:T(1,128)}, f32[3,1,256]{2,1,0:T(1,128)}) custom-call(s32[2,9]{1,0:T(2,128)S(1)} %copy-done.7, bf16[4,80,256]{2,1,0:T(8,128)(2,1)S(1)} %copy-done, f32[3,3,256]{2,1,0:T(4,128)S(1)} %copy-done.3, f32[1,256]{1,0:T(1,128)S(1)} %bitcast.6, s32[1,256]{1,0:T(1,128)S(1)} %bitcast.8, ...), custom_call_target="tpu_custom_call" | custom-call | tf_op jit(solution)/shard_map/pairs/pallas_call | solution.py:373
Async XLA Ops:
  0.6 9.6 %copy-start.6 = (s32[256]{0:T(256)S(1)}, s32[256]{0:T(256)}, u32[]{:S(2)}) copy-start(s32[256]{0:T(256)} %param.17) | copy-start | bytes 3076
  0.6 9.6 %copy-start.7 = (s32[2,9]{1,0:T(2,128)S(1)}, s32[2,9]{1,0:T(2,128)}, u32[]{:S(2)}) copy-start(s32[2,9]{1,0:T(2,128)} %tiles_ref.1) | copy-start | bytes 220
  0.7 9.6 %copy-start.8 = (f32[64]{0:T(128)S(1)}, f32[64]{0:T(128)}, u32[]{:S(2)}) copy-start(f32[64]{0:T(128)} %param.20) | copy-start | bytes 772
  10.2 0.7 %copy-start.4 = (bf16[16,256]{1,0:T(8,128)(2,1)S(1)}, bf16[16,256]{1,0:T(8,128)(2,1)}, u32[]{:S(2)}) copy-start(bf16[16,256]{1,0:T(8,128)(2,1)} %get-tuple-element.12.read) | copy-start | bytes 24580
  10.2 0.7 %copy-start.5 = (f32[256]{0:T(256)S(1)}, f32[256]{0:T(256)}, u32[]{:S(2)}) copy-start(f32[256]{0:T(256)} %param.14) | copy-start | bytes 3076
  10.9 0.9 %copy-start = (bf16[4,80,256]{2,1,0:T(8,128)(2,1)S(1)}, bf16[4,80,256]{2,1,0:T(8,128)(2,1)}, u32[]{:S(2)}) copy-start(bf16[4,80,256]{2,1,0:T(8,128)(2,1)} %get-tuple-element.8.rim_ref) | copy-start | bytes 491524
  11.8 0.8 %copy-start.1 = (bf16[256,128]{1,0:T(8,128)(2,1)S(1)}, bf16[256,128]{1,0:T(8,128)(2,1)}, u32[]{:S(2)}) copy-start(bf16[256,128]{1,0:T(8,128)(2,1)} %get-tuple-element.10.fwd) | copy-start | bytes 196612
  12.6 0.8 %copy-start.2 = (bf16[128,256]{1,0:T(8,128)(2,1)S(1)}, bf16[128,256]{1,0:T(8,128)(2,1)}, u32[]{:S(2)}) copy-start(bf16[128,256]{1,0:T(8,128)(2,1)} %get-tuple-element.11.bwd) | copy-start | bytes 196612
  13.5 0.7 %copy-start.3 = (f32[3,3,256]{2,1,0:T(4,128)S(1)}, f32[3,3,256]{2,1,0:T(4,128)}, u32[]{:S(2)}) copy-start(f32[3,3,256]{2,1,0:T(4,128)} %get-tuple-element.9.state_ref) | copy-start | bytes 27652
where the time goes:
time: 34.5 us; the launch traced here: 34.1 us
  Pallas kernels  29.4 us (85%)
  local copies, waits for them, and re-layouts  3.97 us (12%)
  between operations  0.71 us (2%)
    pallas_call x1, Pallas kernels, body(): pl.pallas_call(functools.partial(pair_kernel, shards, span, first, tile_b...  19.9 us
    pallas_call x1, Pallas kernels, body(): pl.pallas_call(functools.partial(exchange_kernel, shards, beads, span, fi...  9.49 us
    unnamed x18, local copies, waits for them, and re-layouts  3.97 us

commit v1 on v0

--- a/solution.py
+++ b/solution.py
@@ -393,7 +393,6 @@
             pltpu.SMEM((entries,), i32),
             pltpu.SMEM((entries * SEGS + 2,), i32),
         ],
-        compiler_params=pltpu.CompilerParams(vmem_limit_bytes=32 * 1024 * 1024),
         name="pairs",
     )(
         tile_blocks, rim, state, mass_row, slot_row, fwd, bwd, read,

time: 34.5 us -> 29.2 us (0.85)
  the two profiles are of different devices: /device:TPU:8 before, /device:TPU:0 now
where the time goes in v1:
time: 29.2 us; the launch traced here: 29.6 us
  Pallas kernels  28.9 us (99%)
  between operations  0.64 us (2%)
    pallas_call x1, Pallas kernels, body(): pl.pallas_call(functools.partial(pair_kernel, shards, span, first, tile_b...  17.3 us
    pallas_call x1, Pallas kernels, body(): pl.pallas_call(functools.partial(exchange_kernel, shards, beads, span, fi...  11.6 us

profile of v1, /device:TPU:0, one launch (start us, length us, event | category | flops | bytes accessed | tf_op | source)
XLA Modules:
  0.0 29.6 jit_solution(12842077019691728372)
XLA Ops:
  0.6 11.6 %exchange.1 = (bf16[4,80,256]{2,1,0:T(8,128)(2,1)}, f32[3,3,256]{2,1,0:T(4,128)}, bf16[256,128]{1,0:T(8,128)(2,1)}, bf16[128,256]{1,0:T(8,128)(2,1)}, bf16[16,256]{1,0:T(8,128)(2,1)}) custom-call(f32[3,1,256]{2,1,0:T(1,128)} %pos_ref.1, f32[3,1,256]{2,1,0:T(1,128)} %vel_ref.1, f32[3,1,256]{2,1,0:T(1,128)} %force_ref.1, f32[1,256]{1,0:T(1,128)} %bitcast.6, ...), custom_call_target="tpu_custom_call" | custom-call | tf_op jit(solution)/shard_map/exchange/pallas_call | solution.py:349
  12.3 17.3 %pairs.1 = (f32[3,1,256]{2,1,0:T(1,128)}, f32[3,1,256]{2,1,0:T(1,128)}, f32[3,1,256]{2,1,0:T(1,128)}) custom-call(s32[2,9]{1,0:T(2,128)} %tiles_ref.1, bf16[4,80,256]{2,1,0:T(8,128)(2,1)} %get-tuple-element.8.rim_ref, f32[3,3,256]{2,1,0:T(4,128)} %get-tuple-element.9.state_ref, f32[1,256]{1,0:T(1,128)} %bitcast.7, s32[1,256]{1,0:T(1,128)} %bitcast.9, ...), custom_call_target="tpu_custom_call" | custom-call | tf_op jit(solution)/shard_map/pairs/pallas_call | solution.py:373
